TPU v7x, 32 devices: a whole 2x2x4 slice. The times are simulated.
32 devices in a mesh: sub: 8 (over z, x), agg: 4 (over y, core).
Axes of the slice: x: 2, y: 2, z: 4, core: 2. Of those that a mesh axis runs over, the one named last changes fastest.
Arguments:
- dual_load: float32 [4, 8, 64, 1536], P('agg', 'sub'), may hold values from -58 to 58
- interface_inverse: bfloat16 [4, 8, 1536, 1536], P('agg', 'sub'), may hold values from -1 to 2.5, as said below
- dirichlet: bfloat16 [4, 8, 1536, 1536], P('agg', 'sub'), may hold values from -1 to 2.5, as said below
- coupling: bfloat16 [4, 8, 128, 1536], P('agg', 'sub'), may hold values from -0.15625 to 0.15625
- neighbours: int32 [4, 8, 8], P('agg', 'sub'), may hold values from -1 to 7, as said below
- face_counts: int32 [4, 8, 8], P('agg', 'sub'), may hold values from 0 to 192, as said below
- owners: int32 [4, 8, 128, 1], P('agg', 'sub'), may hold values from 0 to 3; in each aligned block of 128 rows (0 to 127, 128 to 255, ..., all dimensions but the last counted through in order) at most 48 rows name the same one
- primal_rows: int32 [4, 8, 128], P('agg', 'sub'), may hold values from 0 to 1023
- coarse_inverse: float32 [4, 1024, 1024], P('agg', 'sub'), may hold values from -1 to 1.5, as said below
Outputs:
- solution: float32 [4, 8, 64, 1536], P('agg', 'sub')
- residual: float32 [4, 8, 64, 1536], P('agg', 'sub')
Inputs may be any that keep to these rules, and one draw needn't show every extreme that they name: `neighbours`: each subdomain lists peers of its own aggregate by their index along sub, -1 in empty slots; no peer twice; if j lists i then i lists j; every listed peer lies within a cyclic distance of 3 along sub. `face_counts`: 0 exactly in empty slots, 48 or more elsewhere; both sides of a face give the same count and hold its rows in the same order. `owners`: among the 128 primal rows of one subdomain no aggregate is named more than 48 times. `interface_inverse`: each subdomain's matrix is symmetric positive definite. `dirichlet`: each subdomain's matrix is symmetric positive definite. `coarse_inverse`: each aggregate's matrix is symmetric positive definite.
All inputs are finite; a program needn't handle non-finite values.
Results may differ from a plain program's by a relative error of at most 0.011.
Values sent between devices are 32-bit elements; how exact they have to be, the bound alone decides.
A program may use at most 128 MiB of HBM per device.

v0:
```python
import jax
import jax.numpy as jnp
from jax import lax
from jax.sharding import PartitionSpec as P

NC = 1024
CAP = 48
ITERS = 2


FULL_PRECISION = lax.Precision.HIGHEST
CONTRACT_LAST = (((1,), (1,)), ((), ()))


def from_behind_2(block, axis, distance):
    devices = range(lax.axis_size(axis))
    route = [((i - distance) % len(devices), i) for i in devices]
    return lax.ppermute(block, axis, route)


def shards(
    dual_load,
    interface_inverse,
    dirichlet,
    coupling,
    neighbours,
    face_counts,
    owners,
    primal_rows,
    coarse_inverse,
):
    inverse_block = interface_inverse[0, 0]
    dirichlet_block = dirichlet[0, 0]
    coupling_block = coupling[0, 0]
    peer_list = neighbours[0, 0]
    count_list = face_counts[0, 0]
    sub_count = lax.axis_size("sub")
    agg_count = lax.axis_size("agg")
    position = lax.axis_index("sub")
    slot_count = peer_list.shape[0]
    inner_order = inverse_block.shape[0]
    face_depth = inner_order // slot_count
    reach = min(4, (sub_count - 1) // 2)
    inside = (
        (jnp.arange(face_depth, dtype=jnp.int32)[None, :] < count_list[:, None])
        .reshape(1, inner_order)
        .astype(jnp.float32)
    )

    def assemble(local):
        case_count = local.shape[0]
        faces = local.reshape(case_count, slot_count, face_depth)
        placed = jnp.zeros_like(faces)
        for distance in range(1, reach + 1):
            ahead = (position + distance) % sub_count
            behind = (position + sub_count - distance) % sub_count
            to_ahead = (peer_list == ahead).astype(jnp.float32)[None, :, None]
            to_behind = (peer_list == behind).astype(jnp.float32)[None, :, None]
            upward = jnp.sum(faces * to_ahead, axis=1)
            downward = jnp.sum(faces * to_behind, axis=1)
            from_behind = from_behind_2(upward, "sub", distance)
            from_ahead = from_behind_2(downward, "sub", -distance)
            placed = (
                placed + to_behind * from_behind[:, None, :] + to_ahead * from_ahead[:, None, :]
            )
        return inside * (local + placed.reshape(case_count, inner_order))

    owner_ids = owners[0, 0, :, 0]
    row_ids = primal_rows[0, 0]
    owner_hot = (owner_ids[:, None] == jnp.arange(agg_count, dtype=jnp.int32)[None, :]).astype(
        jnp.int32
    )
    earlier = jnp.cumsum(owner_hot, axis=0) - owner_hot
    owner_rank = jnp.sum(earlier * owner_hot, axis=1)
    slot_index = owner_ids * CAP + owner_rank
    packing = slot_index[:, None] == jnp.arange(agg_count * CAP, dtype=jnp.int32)[None, :]
    packing_float = packing.astype(jnp.float32)
    sent_rows = jnp.sum(packing.astype(jnp.int32) * (row_ids[:, None] + 1), axis=0) - 1
    got_rows = lax.all_to_all(sent_rows, "agg", split_axis=0, concat_axis=0, tiled=True)
    scatter_hot = (got_rows[:, None] == jnp.arange(NC, dtype=jnp.int32)[None, :]).astype(
        jnp.float32
    )
    inverse_rows = coarse_inverse[0]

    def precondition(field):
        packed = field.astype(jnp.bfloat16)
        return assemble(
            inside * jnp.dot(packed, dirichlet_block, preferred_element_type=jnp.float32)
        )

    def residual_norm(first, second):
        return lax.psum(jnp.sum(first * second, axis=1), ("sub", "agg"))

    rhs = assemble(inside * dual_load[0, 0])
    solution = jnp.zeros_like(rhs)
    residual = rhs
    precond = precondition(residual)
    direction = precond
    residual_dot = residual_norm(residual, precond)
    for iteration in range(ITERS):
        operator_packed = direction.astype(jnp.bfloat16)
        own = jnp.dot(operator_packed, inverse_block, preferred_element_type=jnp.float32)
        terms = lax.dot_general(
            operator_packed, coupling_block, CONTRACT_LAST, preferred_element_type=jnp.float32
        )
        outgoing = jnp.dot(terms, packing_float, precision=FULL_PRECISION)
        gathered = jnp.dot(
            lax.all_to_all(outgoing, "agg", split_axis=1, concat_axis=1, tiled=True),
            scatter_hot,
            precision=FULL_PRECISION,
        )
        coarse_rhs = lax.psum(gathered, "sub")
        partial_rows = lax.dot_general(
            coarse_rhs, inverse_rows, CONTRACT_LAST, precision=FULL_PRECISION
        )
        coarse_sol = lax.all_gather(partial_rows, "sub", axis=1, tiled=True)
        answer = lax.dot_general(coarse_sol, scatter_hot, CONTRACT_LAST, precision=FULL_PRECISION)
        returned = lax.all_to_all(answer, "agg", split_axis=1, concat_axis=1, tiled=True)
        local_back = lax.dot_general(
            returned, packing_float, CONTRACT_LAST, precision=FULL_PRECISION
        )
        correction = jnp.dot(
            local_back.astype(jnp.bfloat16), coupling_block, preferred_element_type=jnp.float32
        )
        image = assemble(inside * (own + correction))
        alpha = (residual_dot / lax.psum(jnp.sum(direction * image, axis=1), ("sub", "agg")))[
            :, None
        ]
        solution = solution + alpha * direction
        residual = residual - alpha * image
        if iteration + 1 < ITERS:
            precond = precondition(residual)
            next_dot = residual_norm(residual, precond)
            direction = precond + (next_dot / residual_dot)[:, None] * direction
            residual_dot = next_dot
    return (solution[None, None], residual[None, None])


def solution(mesh):
    in_specs = (
        P("agg", "sub", None, None),
        P("agg", "sub", None, None),
        P("agg", "sub", None, None),
        P("agg", "sub", None, None),
        P("agg", "sub", None),
        P("agg", "sub", None),
        P("agg", "sub", None, None),
        P("agg", "sub", None),
        P("agg", "sub", None),
    )
    out_specs = (P("agg", "sub", None, None), P("agg", "sub", None, None))
    return jax.shard_map(shards, mesh=mesh, in_specs=in_specs, out_specs=out_specs, check_vma=False)
```

profile of v0, /device:TPU:0, one launch (start us, length us, event | category | flops | bytes accessed | tf_op | source)
XLA Modules:
  0.0 557.0 jit_solution(9417829108767460508)
XLA Ops:
  11.2 2.9 collective-permute-start
  14.2 3.0 collective-permute-start.1
  17.2 3.8 collective-permute-start.3
  24.0 2.2 collective-permute-done.5
  40.8 4.1 fusion.8
  54.4 3.3 collective-permute-start.9
  59.0 3.7 all-to-all-start.1
  86.7 3.3 all-to-all-start
  98.7 71.5 %all-reduce.4.cloned.1.call-done = f32[64,1024]{1,0:T(8,128)} async-done(((f32[64,1024]{1,0:T(8,128)}), f32[64,1024]{1,0:T(8,128)}) %all-reduce.4.cloned.1.call-update) | async-done | bytes 262160 | tf_op jit(solution)/shard_map/psum | solution.py:112
  171.9 30.9 %all_gather.6 = f32[64,1024]{1,0:T(8,128)S(1)} all-gather(f32[64,128]{1,0:T(8,128)S(1)} %fusion.32), channel_id=1, replica_groups=mesh['sub'=8,'agg'=4] {'sub'}, dimensions={1}, use_global_device_ids=true | all-gather | bytes 294912 | tf_op jit(solution)/shard_map/all_gather | solution.py:116
  205.6 6.5 %all_to_all.54 = f32[4,1,3072]{2,1,0:T(1,128)S(1)} all-to-all(f32[4,1,3072]{2,1,0:T(1,128)S(1)} %reshape.532), channel_id=1, replica_groups=mesh['sub'=8,'agg'=4] {'agg'}, dimensions={0} | all-to-all | bytes 98304 | tf_op jit(solution)/shard_map/all_to_all | solution.py:118
  215.5 4.0 fusion.23
  221.5 2.8 multiply_reduce_fusion.17
  224.3 2.6 collective-permute-start.13
  226.9 3.8 collective-permute-start.15
  230.8 3.8 collective-permute-start.17
  254.1 3.4 multiply_reduce_fusion.32
  257.5 38.5 %all-reduce = (f32[64]{0:T(128)S(1)}, f32[64]{0:T(128)S(1)}) all-reduce(f32[64]{0:T(128)S(1)} %get-tuple-element.33, f32[64]{0:T(128)S(1)} %get-tuple-element.32), channel_id=1, replica_groups=mesh['sub'=8,'agg'=4] {'sub','agg'}, use_global_device_ids=true, to_apply=%region_13.14 | all-reduce | flops 128 | bytes 1024 | tf_op jit(solution)/shard_map/psum | solution.py:92
  297.1 3.3 fusion.11
  302.0 3.2 collective-permute-start.19
  305.7 3.3 collective-permute-start.21
  309.0 3.8 collective-permute-start.23
  323.4 39.3 %psum.45 = f32[64]{0:T(128)S(1)} all-reduce(f32[64]{0:T(128)S(1)} %get-tuple-element.38), channel_id=1, replica_groups=mesh['sub'=8,'agg'=4] {'sub','agg'}, use_global_device_ids=true, to_apply=%region_33.34 | all-reduce | flops 64 | bytes 512 | tf_op jit(solution)/shard_map/psum | solution.py:92
  364.6 7.4 %all_to_all.55 = f32[4,1,3072]{2,1,0:T(1,128)S(1)} all-to-all(f32[4,1,3072]{2,1,0:T(1,128)S(1)} %reshape.534), channel_id=1, replica_groups=mesh['sub'=8,'agg'=4] {'agg'}, dimensions={0} | all-to-all | bytes 98304 | tf_op jit(solution)/shard_map/all_to_all | solution.py:108
  374.7 70.1 %all-reduce.6.cloned.1.call-done = f32[64,1024]{1,0:T(8,128)} async-done(((f32[64,1024]{1,0:T(8,128)}), f32[64,1024]{1,0:T(8,128)}) %all-reduce.6.cloned.1.call-update) | async-done | bytes 262160 | tf_op jit(solution)/shard_map/psum | solution.py:112
  446.5 30.8 %all_gather.7 = f32[64,1024]{1,0:T(8,128)S(1)} all-gather(f32[64,128]{1,0:T(8,128)S(1)} %fusion.30), channel_id=1, replica_groups=mesh['sub'=8,'agg'=4] {'sub'}, dimensions={1}, use_global_device_ids=true | all-gather | bytes 294912 | tf_op jit(solution)/shard_map/all_gather | solution.py:116
  478.0 6.6 %all_to_all.56 = f32[4,1,3072]{2,1,0:T(1,128)S(1)} all-to-all(f32[4,1,3072]{2,1,0:T(1,128)S(1)} %reshape.536), channel_id=1, replica_groups=mesh['sub'=8,'agg'=4] {'agg'}, dimensions={0} | all-to-all | bytes 98304 | tf_op jit(solution)/shard_map/all_to_all | solution.py:118
  485.9 3.3 fusion.20
  490.8 2.6 collective-permute-start.25
  493.3 3.8 collective-permute-start.27
  497.2 3.8 collective-permute-start.29
  511.5 37.6 %psum.47 = f32[64]{0:T(128)S(1)} all-reduce(f32[64]{0:T(128)S(1)} %get-tuple-element.36), channel_id=1, replica_groups=mesh['sub'=8,'agg'=4] {'sub','agg'}, use_global_device_ids=true, to_apply=%region_42.43 | all-reduce | flops 64 | bytes 512 | tf_op jit(solution)/shard_map/psum | solution.py:126
  (255 shorter events, 129.1 us)
Async XLA Ops:
  11.2 26.7 %collective-permute-start = (f32[64,192]{1,0:T(8,128)S(1)}, f32[64,192]{1,0:T(8,128)S(1)}, u32[]{:S(2)}, u32[]{:S(2)}) collective-permute-start(f32[64,192]{1,0:T(8,128)S(1)} %get-tuple-element.2), channel_id=1, source_target_pairs={{28,0},{0,4},{4,8},{8,12},{12,16},{16,20},{20,24},{24,28},{29,1},{... | collective-permute-start | bytes 147464 | tf_op jit(solution)/shard_map/ppermute | solution.py:18
  14.2 21.0 %collective-permute-start.1 = (f32[64,192]{1,0:T(8,128)}, f32[64,192]{1,0:T(8,128)S(1)}, u32[]{:S(2)}, u32[]{:S(2)}) collective-permute-start(f32[64,192]{1,0:T(8,128)} %get-tuple-element.3), channel_id=1, source_target_pairs={{4,0},{8,4},{12,8},{16,12},{20,16},{24,20},{28,24},{0,28},{5,1},{9... | collective-permute-start | bytes 147464 | tf_op jit(solution)/shard_map/ppermute | solution.py:18
  17.2 17.0 %collective-permute-start.2 = (f32[64,192]{1,0:T(8,128)S(1)}, f32[64,192]{1,0:T(8,128)S(1)}, u32[]{:S(2)}, u32[]{:S(2)}) collective-permute-start(f32[64,192]{1,0:T(8,128)S(1)} %get-tuple-element.4), channel_id=1, source_target_pairs={{24,0},{28,4},{0,8},{4,12},{8,16},{12,20},{16,24},{20,28},{25,1},{... | collective-permute-start | bytes 147464 | tf_op jit(solution)/shard_map/ppermute | solution.py:18
  17.2 16.0 %collective-permute-start.3 = (f32[64,192]{1,0:T(8,128)S(1)}, f32[64,192]{1,0:T(8,128)S(1)}, u32[]{:S(2)}, u32[]{:S(2)}) collective-permute-start(f32[64,192]{1,0:T(8,128)S(1)} %get-tuple-element.5), channel_id=1, source_target_pairs={{8,0},{12,4},{16,8},{20,12},{24,16},{28,20},{0,24},{4,28},{9,1},{1... | collective-permute-start | bytes 147464 | tf_op jit(solution)/shard_map/ppermute | solution.py:18
  48.0 9.6 %collective-permute-start.7 = (f32[64,192]{1,0:T(8,128)S(1)}, f32[64,192]{1,0:T(8,128)S(1)}, u32[]{:S(2)}, u32[]{:S(2)}) collective-permute-start(f32[64,192]{1,0:T(8,128)S(1)} %get-tuple-element.31), channel_id=1, source_target_pairs={{4,0},{8,4},{12,8},{16,12},{20,16},{24,20},{28,24},{0,28},{5,1},{9... | collective-permute-start | bytes 147464 | tf_op jit(solution)/shard_map/ppermute | solution.py:18
  50.9 29.2 %collective-permute-start.6 = (f32[64,192]{1,0:T(8,128)S(1)}, f32[64,192]{1,0:T(8,128)S(1)}, u32[]{:S(2)}, u32[]{:S(2)}) collective-permute-start(f32[64,192]{1,0:T(8,128)S(1)} %get-tuple-element.26), channel_id=1, source_target_pairs={{28,0},{0,4},{4,8},{8,12},{12,16},{16,20},{20,24},{24,28},{29,1},{... | collective-permute-start | bytes 147464 | tf_op jit(solution)/shard_map/ppermute | solution.py:18
  51.4 25.9 %collective-permute-start.11 = (f32[64,192]{1,0:T(8,128)S(1)}, f32[64,192]{1,0:T(8,128)S(1)}, u32[]{:S(2)}, u32[]{:S(2)}) collective-permute-start(f32[64,192]{1,0:T(8,128)S(1)} %get-tuple-element.27), channel_id=1, source_target_pairs={{12,0},{16,4},{20,8},{24,12},{28,16},{0,20},{4,24},{8,28},{13,1},{... | collective-permute-start | bytes 147464 | tf_op jit(solution)/shard_map/ppermute | solution.py:18
  52.7 20.9 %collective-permute-start.10 = (f32[64,192]{1,0:T(8,128)S(1)}, f32[64,192]{1,0:T(8,128)}, u32[]{:S(2)}, u32[]{:S(2)}) collective-permute-start(f32[64,192]{1,0:T(8,128)S(1)} %get-tuple-element.28), channel_id=1, source_target_pairs={{20,0},{24,4},{28,8},{0,12},{4,16},{8,20},{12,24},{16,28},{21,1},{... | collective-permute-start | bytes 147464 | tf_op jit(solution)/shard_map/ppermute | solution.py:18
  54.4 15.6 %collective-permute-start.9 = (f32[64,192]{1,0:T(8,128)S(1)}, f32[64,192]{1,0:T(8,128)}, u32[]{:S(2)}, u32[]{:S(2)}) collective-permute-start(f32[64,192]{1,0:T(8,128)S(1)} %get-tuple-element.29), channel_id=1, source_target_pairs={{8,0},{12,4},{16,8},{20,12},{24,16},{28,20},{0,24},{4,28},{9,1},{1... | collective-permute-start | bytes 147464 | tf_op jit(solution)/shard_map/ppermute | solution.py:18
  57.6 8.6 %collective-permute-start.8 = (f32[64,192]{1,0:T(8,128)S(1)}, f32[64,192]{1,0:T(8,128)}, u32[]{:S(2)}, u32[]{:S(2)}) collective-permute-start(f32[64,192]{1,0:T(8,128)S(1)} %get-tuple-element.30), channel_id=1, source_target_pairs={{24,0},{28,4},{0,8},{4,12},{8,16},{12,20},{16,24},{20,28},{25,1},{... | collective-permute-start | bytes 147464 | tf_op jit(solution)/shard_map/ppermute | solution.py:18
  59.0 27.7 %all-to-all-start.1 = ((s32[4,48,1]{1,2,0:T(1,128)}), s32[4,48,1]{1,2,0:T(1,128)}, u32[]{:S(2)}, u32[]{:S(2)}) async-start(s32[4,48,1]{1,2,0:T(1,128)} %bitcast.16), calls=%async_computation.1 | async-start | bytes 4096 | tf_op jit(solution)/shard_map/all_to_all | solution.py:79
  86.7 7.3 %all-to-all-start = ((f32[4,1,3072]{2,1,0:T(1,128)}), f32[4,1,3072]{2,1,0:T(1,128)S(1)}, u32[]{:S(2)}, u32[]{:S(2)}) async-start(f32[4,1,3072]{2,1,0:T(1,128)} %reshape.530), calls=%async_computation | async-start | bytes 98304 | tf_op jit(solution)/shard_map/all_to_all | solution.py:108
  90.0 80.3 %all-reduce.4.cloned.1.call-start = ((), (), s32[]{:S(2)}) async-start(), calls=%async_computation.5 | async-start | bytes 524288 | tf_op jit(solution)/shard_map/psum | solution.py:112
  98.7 346.2 %all-reduce.6.cloned.1.call-start = ((), (), s32[]{:S(2)}) async-start(), calls=%async_computation.6 | async-start | bytes 524288 | tf_op jit(solution)/shard_map/psum | solution.py:112
  224.3 10.3 %collective-permute-start.13 = (f32[64,192]{1,0:T(8,128)S(1)}, f32[64,192]{1,0:T(8,128)S(1)}, u32[]{:S(2)}, u32[]{:S(2)}) collective-permute-start(f32[64,192]{1,0:T(8,128)S(1)} %get-tuple-element.25), channel_id=1, source_target_pairs={{4,0},{8,4},{12,8},{16,12},{20,16},{24,20},{28,24},{0,28},{5,1},{9... | collective-permute-start | bytes 147464 | tf_op jit(solution)/shard_map/ppermute | solution.py:18
  226.9 18.1 %collective-permute-start.14 = (f32[64,192]{1,0:T(8,128)}, f32[64,192]{1,0:T(8,128)}, u32[]{:S(2)}, u32[]{:S(2)}) collective-permute-start(f32[64,192]{1,0:T(8,128)} %get-tuple-element.24), channel_id=1, source_target_pairs={{24,0},{28,4},{0,8},{4,12},{8,16},{12,20},{16,24},{20,28},{25,1},{... | collective-permute-start | bytes 147464 | tf_op jit(solution)/shard_map/ppermute | solution.py:18
  226.9 19.9 %collective-permute-start.15 = (f32[64,192]{1,0:T(8,128)}, f32[64,192]{1,0:T(8,128)}, u32[]{:S(2)}, u32[]{:S(2)}) collective-permute-start(f32[64,192]{1,0:T(8,128)} %get-tuple-element.23), channel_id=1, source_target_pairs={{8,0},{12,4},{16,8},{20,12},{24,16},{28,20},{0,24},{4,28},{9,1},{1... | collective-permute-start | bytes 147464 | tf_op jit(solution)/shard_map/ppermute | solution.py:18
  230.8 17.9 %collective-permute-start.16 = (f32[64,192]{1,0:T(8,128)}, f32[64,192]{1,0:T(8,128)}, u32[]{:S(2)}, u32[]{:S(2)}) collective-permute-start(f32[64,192]{1,0:T(8,128)} %get-tuple-element.22), channel_id=1, source_target_pairs={{20,0},{24,4},{28,8},{0,12},{4,16},{8,20},{12,24},{16,28},{21,1},{... | collective-permute-start | bytes 147464 | tf_op jit(solution)/shard_map/ppermute | solution.py:18
  230.8 19.7 %collective-permute-start.17 = (f32[64,192]{1,0:T(8,128)}, f32[64,192]{1,0:T(8,128)}, u32[]{:S(2)}, u32[]{:S(2)}) collective-permute-start(f32[64,192]{1,0:T(8,128)} %get-tuple-element.21), channel_id=1, source_target_pairs={{12,0},{16,4},{20,8},{24,12},{28,16},{0,20},{4,24},{8,28},{13,1},{... | collective-permute-start | bytes 147464 | tf_op jit(solution)/shard_map/ppermute | solution.py:18
  235.2 17.1 %collective-permute-start.12 = (f32[64,192]{1,0:T(8,128)S(1)}, f32[64,192]{1,0:T(8,128)}, u32[]{:S(2)}, u32[]{:S(2)}) collective-permute-start(f32[64,192]{1,0:T(8,128)S(1)} %get-tuple-element.20), channel_id=1, source_target_pairs={{28,0},{0,4},{4,8},{8,12},{12,16},{16,20},{20,24},{24,28},{29,1},{... | collective-permute-start | bytes 147464 | tf_op jit(solution)/shard_map/ppermute | solution.py:18
  302.0 10.9 %collective-permute-start.19 = (f32[64,192]{1,0:T(8,128)S(1)}, f32[64,192]{1,0:T(8,128)S(1)}, u32[]{:S(2)}, u32[]{:S(2)}) collective-permute-start(f32[64,192]{1,0:T(8,128)S(1)} %get-tuple-element.19), channel_id=1, source_target_pairs={{4,0},{8,4},{12,8},{16,12},{20,16},{24,20},{28,24},{0,28},{5,1},{9... | collective-permute-start | bytes 147464 | tf_op jit(solution)/shard_map/ppermute | solution.py:18
  305.2 7.9 %collective-permute-start.20 = (f32[64,192]{1,0:T(8,128)S(1)}, f32[64,192]{1,0:T(8,128)S(1)}, u32[]{:S(2)}, u32[]{:S(2)}) collective-permute-start(f32[64,192]{1,0:T(8,128)S(1)} %get-tuple-element.18), channel_id=1, source_target_pairs={{24,0},{28,4},{0,8},{4,12},{8,16},{12,20},{16,24},{20,28},{25,1},{... | collective-permute-start | bytes 147464 | tf_op jit(solution)/shard_map/ppermute | solution.py:18
  305.7 7.6 %collective-permute-start.21 = (f32[64,192]{1,0:T(8,128)}, f32[64,192]{1,0:T(8,128)}, u32[]{:S(2)}, u32[]{:S(2)}) collective-permute-start(f32[64,192]{1,0:T(8,128)} %get-tuple-element.17), channel_id=1, source_target_pairs={{8,0},{12,4},{16,8},{20,12},{24,16},{28,20},{0,24},{4,28},{9,1},{1... | collective-permute-start | bytes 147464 | tf_op jit(solution)/shard_map/ppermute | solution.py:18
  309.0 6.4 %collective-permute-start.22 = (f32[64,192]{1,0:T(8,128)}, f32[64,192]{1,0:T(8,128)}, u32[]{:S(2)}, u32[]{:S(2)}) collective-permute-start(f32[64,192]{1,0:T(8,128)} %get-tuple-element.16), channel_id=1, source_target_pairs={{20,0},{24,4},{28,8},{0,12},{4,16},{8,20},{12,24},{16,28},{21,1},{... | collective-permute-start | bytes 147464 | tf_op jit(solution)/shard_map/ppermute | solution.py:18
  309.0 8.2 %collective-permute-start.23 = (f32[64,192]{1,0:T(8,128)}, f32[64,192]{1,0:T(8,128)}, u32[]{:S(2)}, u32[]{:S(2)}) collective-permute-start(f32[64,192]{1,0:T(8,128)} %get-tuple-element.15), channel_id=1, source_target_pairs={{12,0},{16,4},{20,8},{24,12},{28,16},{0,20},{4,24},{8,28},{13,1},{... | collective-permute-start | bytes 147464 | tf_op jit(solution)/shard_map/ppermute | solution.py:18
  312.8 7.1 %collective-permute-start.18 = (f32[64,192]{1,0:T(8,128)S(1)}, f32[64,192]{1,0:T(8,128)}, u32[]{:S(2)}, u32[]{:S(2)}) collective-permute-start(f32[64,192]{1,0:T(8,128)S(1)} %get-tuple-element.14), channel_id=1, source_target_pairs={{28,0},{0,4},{4,8},{8,12},{12,16},{16,20},{20,24},{24,28},{29,1},{... | collective-permute-start | bytes 147464 | tf_op jit(solution)/shard_map/ppermute | solution.py:18
  490.8 10.2 %collective-permute-start.25 = (f32[64,192]{1,0:T(8,128)S(1)}, f32[64,192]{1,0:T(8,128)S(1)}, u32[]{:S(2)}, u32[]{:S(2)}) collective-permute-start(f32[64,192]{1,0:T(8,128)S(1)} %get-tuple-element.13), channel_id=1, source_target_pairs={{4,0},{8,4},{12,8},{16,12},{20,16},{24,20},{28,24},{0,28},{5,1},{9... | collective-permute-start | bytes 147464 | tf_op jit(solution)/shard_map/ppermute | solution.py:18
  493.3 8.2 %collective-permute-start.26 = (f32[64,192]{1,0:T(8,128)S(1)}, f32[64,192]{1,0:T(8,128)S(1)}, u32[]{:S(2)}, u32[]{:S(2)}) collective-permute-start(f32[64,192]{1,0:T(8,128)S(1)} %get-tuple-element.12), channel_id=1, source_target_pairs={{24,0},{28,4},{0,8},{4,12},{8,16},{12,20},{16,24},{20,28},{25,1},{... | collective-permute-start | bytes 147464 | tf_op jit(solution)/shard_map/ppermute | solution.py:18
  493.3 8.5 %collective-permute-start.27 = (f32[64,192]{1,0:T(8,128)}, f32[64,192]{1,0:T(8,128)}, u32[]{:S(2)}, u32[]{:S(2)}) collective-permute-start(f32[64,192]{1,0:T(8,128)} %get-tuple-element.11), channel_id=1, source_target_pairs={{8,0},{12,4},{16,8},{20,12},{24,16},{28,20},{0,24},{4,28},{9,1},{1... | collective-permute-start | bytes 147464 | tf_op jit(solution)/shard_map/ppermute | solution.py:18
  497.2 6.5 %collective-permute-start.28 = (f32[64,192]{1,0:T(8,128)}, f32[64,192]{1,0:T(8,128)}, u32[]{:S(2)}, u32[]{:S(2)}) collective-permute-start(f32[64,192]{1,0:T(8,128)} %get-tuple-element.10), channel_id=1, source_target_pairs={{20,0},{24,4},{28,8},{0,12},{4,16},{8,20},{12,24},{16,28},{21,1},{... | collective-permute-start | bytes 147464 | tf_op jit(solution)/shard_map/ppermute | solution.py:18
  497.2 8.3 %collective-permute-start.29 = (f32[64,192]{1,0:T(8,128)}, f32[64,192]{1,0:T(8,128)}, u32[]{:S(2)}, u32[]{:S(2)}) collective-permute-start(f32[64,192]{1,0:T(8,128)} %get-tuple-element.9), channel_id=1, source_target_pairs={{12,0},{16,4},{20,8},{24,12},{28,16},{0,20},{4,24},{8,28},{13,1},{... | collective-permute-start | bytes 147464 | tf_op jit(solution)/shard_map/ppermute | solution.py:18
  501.0 7.1 %collective-permute-start.24 = (f32[64,192]{1,0:T(8,128)S(1)}, f32[64,192]{1,0:T(8,128)}, u32[]{:S(2)}, u32[]{:S(2)}) collective-permute-start(f32[64,192]{1,0:T(8,128)S(1)} %get-tuple-element.8), channel_id=1, source_target_pairs={{28,0},{0,4},{4,8},{8,12},{12,16},{16,20},{20,24},{24,28},{29,1},{... | collective-permute-start | bytes 147464 | tf_op jit(solution)/shard_map/ppermute | solution.py:18
  (35 other events, 1132.4 us)
Sparse Core Ops, SparseCore 0:
  98.8 71.3 all-reduce.3
  374.9 69.9 all-reduce.5
where the time goes:
time: 560 us; the launch traced here: 557 us
  blocking collectives  198 us (35%)
  waiting for transfers between devices  149 us (27%)
  local copies, waits for them, and re-layouts  76.6 us (14%)
  starting transfers between devices  58.8 us (10%)
  other arithmetic  32.5 us (6%)
  matrix products  27.5 us (5%)
  between operations  14.8 us (3%)
    psum x2, waiting for transfers between devices, shards(): coarse_rhs = lax.psum(gathered, 'sub')  142 us
    psum x2, blocking collectives, residual_norm(): return lax.psum(jnp.sum(first * second, axis=1), ('sub', 'agg'))  77.8 us
    all_gather x2, blocking collectives, shards(): coarse_sol = lax.all_gather(partial_rows, 'sub', axis=1, tiled=True)  61.7 us
    ppermute x30, starting transfers between devices, from_behind_2(): return lax.ppermute(block, axis, route)  51.8 us
    psum x1, blocking collectives, shards(): lax.psum(jnp.sum(direction * image, axis=1), ('sub', 'agg'))  37.6 us
    mul x39, local copies, waits for them, and re-layouts, assemble(): to_behind * from_behind[:, None, :]  32.2 us
    mul x33, local copies, waits for them, and re-layouts, assemble(): to_ahead * from_ahead[:, None, :]  31.7 us
    all_to_all x2, blocking collectives, shards(): lax.all_to_all(answer, 'agg', split_axis=1, concat_axis=1, tiled=True)  13.1 us
  transfers between devices with their start and end apart: 34, of which 8 were waited for; matrix products, arithmetic and copies ran while one was open for 12% of the time, Pallas kernels for 0%

commit v1 on v0

v1 whole, which is shorter than its diff:
```python
import functools

import jax
import jax.numpy as jnp
from jax import lax
from jax.experimental import pallas as pl
from jax.experimental.pallas import tpu as pltpu
from jax.sharding import PartitionSpec as P

CAP = 48
ITERS = 2
MESH = pl.DeviceIdType.MESH
F32 = jnp.float32
BF16 = jnp.bfloat16
NT = (((1,), (1,)), ((), ()))


def dot(left, right):
    return jnp.dot(left, right, preferred_element_type=F32)


def pack(face):
    cases, depth = face.shape
    whole = depth // 128 * 128
    half = cases // 2
    parts = [face[:, at : at + 128] for at in range(0, whole, 128)]
    if depth > whole:
        parts.append(jnp.concatenate([face[:half, whole:], face[half:, whole:]], axis=1))
    return jnp.concatenate(parts, axis=0)


def unpack(rows, cases, depth):
    whole = depth // 128 * 128
    parts = [rows[at * cases : (at + 1) * cases] for at in range(whole // 128)]
    if depth > whole:
        last = rows[whole // 128 * cases :]
        wide = depth - whole
        parts.append(jnp.concatenate([last[:, :wide], last[:, wide:]], axis=0))
    return jnp.concatenate(parts, axis=1)


def kernel(
    ns,
    na,
    reach,
    dual_ref,
    inverse_hbm,
    dirichlet_hbm,
    coupling_ref,
    peers_ref,
    counts_ref,
    owners_ref,
    rows_ref,
    coarse_ref,
    solution_ref,
    residual_ref,
    inverse_ref,
    dirichlet_ref,
    local_ref,
    field_ref,
    direction_ref,
    packed_ref,
    face_out,
    face_in,
    face_ss,
    face_rs,
    load_sem,
    cp_ref,
    mask_ref,
    ida_out,
    ida_in,
    ida_ss,
    ida_rs,
    idb_out,
    idb_in,
    idb_ss,
    idb_rs,
    hi_ref,
    lo_ref,
    pick_ref,
    a_out,
    a_in,
    a_ss,
    a_rs,
    b_out,
    b_in,
    b_ss,
    b_rs,
    s_out,
    s_in,
    s_ss,
    s_rs,
    r_out,
    r_in,
    r_ss,
    r_rs,
    du_out,
    du_in,
    du_ss,
    du_rs,
    dv_out,
    dv_in,
    dv_ss,
    dv_rs,
):
    cases, order = dual_ref.shape
    slots = peers_ref.shape[0]
    depth = order // slots
    primal = coupling_ref.shape[0]
    crow, nc = coarse_ref.shape
    half = CAP // 2
    used = na * half
    wide = ida_in.shape[2]
    sub = lax.axis_index("sub")
    agg = lax.axis_index("agg")

    def start(axis, src_of, dst, ss, rs):
        me, n = (sub, ns) if axis == "sub" else (agg, na)

        @pl.loop(1, n)
        def _(t):
            peer = lax.rem(me + t, n)
            pltpu.make_async_remote_copy(
                src_ref=src_of(peer),
                dst_ref=dst.at[me],
                send_sem=ss.at[t - 1],
                recv_sem=rs.at[t - 1],
                device_id={axis: peer},
                device_id_type=MESH,
            ).start()

    def receive(axis, src_of, dst, ss, rs):
        me, n = (sub, ns) if axis == "sub" else (agg, na)

        @pl.loop(1, n)
        def _(t):
            peer = lax.rem(me - t + n, n)
            copy = pltpu.make_async_remote_copy(
                src_ref=src_of(peer),
                dst_ref=dst.at[peer],
                send_sem=ss.at[t - 1],
                recv_sem=rs.at[t - 1],
                device_id={axis: peer},
                device_id_type=MESH,
            )
            copy.wait_recv()
            copy.wait_send()

    barrier = pltpu.get_barrier_semaphore()
    for axis, me, n in (("sub", sub, ns), ("agg", agg, na)):

        @pl.loop(1, n)
        def _(t, axis=axis, me=me, n=n):
            pl.semaphore_signal(
                barrier, inc=1, device_id={axis: lax.rem(me + t, n)}, device_id_type=MESH
            )

    load_d = pltpu.make_async_copy(dirichlet_hbm, dirichlet_ref, load_sem.at[0])
    load_k = pltpu.make_async_copy(inverse_hbm, inverse_ref, load_sem.at[1])
    load_d.start()
    load_k.start()

    lane = lax.broadcasted_iota(jnp.int32, (1, order), 1)
    mask = jnp.zeros((1, order), F32)
    for k in range(slots):
        inside = (lane >= k * depth) & (lane < k * depth + counts_ref[k])
        mask = mask + jnp.where(inside, 1.0, 0.0)
    mask_ref[...] = jnp.broadcast_to(mask, mask_ref.shape)

    hops = []
    for distance in range(1, reach + 1):
        ahead = lax.rem(sub + distance, ns)
        behind = lax.rem(sub + ns - distance, ns)
        hops.append((ahead, behind))
        hops.append((behind, ahead))
    weights = [
        [jnp.where(peers_ref[k] == to, 1.0, 0.0) for k in range(slots)] for to, _ in hops
    ]

    def face_copy(phase, e):
        return pltpu.make_async_remote_copy(
            src_ref=face_out.at[phase, e],
            dst_ref=face_in.at[phase, e],
            send_sem=face_ss.at[phase, e],
            recv_sem=face_rs.at[phase, e],
            device_id={"sub": hops[e][0]},
            device_id_type=MESH,
        )

    def faces_start(phase):
        for k in range(slots):
            packed_ref[k] = pack(local_ref[:, k * depth : (k + 1) * depth])
        for e in reversed(range(len(hops))):
            total = weights[e][0] * packed_ref[0]
            for k in range(1, slots):
                total = total + weights[e][k] * packed_ref[k]
            face_out[phase, e] = total
            face_copy(phase, e).start()

    def faces_end(phase, out_ref):
        for e in range(len(hops)):
            face_copy(phase, e).wait()
        for k in range(0, slots, 2):
            pair = []
            for j in (k, k + 1):
                total = weights[1][j] * face_in[phase, 0]
                for e in range(1, len(hops)):
                    total = total + weights[e ^ 1][j] * face_in[phase, e]
                pair.append(unpack(total, cases, depth))
            at = slice(k * depth, (k + 2) * depth)
            out_ref[:, at] = mask_ref[0:1, at] * (
                local_ref[:, at] + jnp.concatenate(pair, axis=1)
            )

    line = lax.broadcasted_iota(jnp.int32, (cases, 2 * cases), 1)
    case = lax.broadcasted_iota(jnp.int32, (cases, 2 * cases), 0)

    def dots_start(phase, first, second):
        spread = jnp.where(line == case, first, 0.0) + jnp.where(
            line == case + cases, second, 0.0
        )
        total = jnp.sum(spread, axis=0, keepdims=True)
        du_out[phase] = jnp.broadcast_to(total, du_out.shape[1:])
        du_in[phase, sub] = du_out[phase]
        start("sub", lambda p: du_out.at[phase], du_in.at[phase], du_ss.at[phase], du_rs.at[phase])

    def dots_turn(phase):
        receive(
            "sub", lambda p: du_out.at[phase], du_in.at[phase], du_ss.at[phase], du_rs.at[phase]
        )
        dv_out[phase] = jnp.sum(du_in[phase], axis=0)
        dv_in[phase, agg] = dv_out[phase]
        start("agg", lambda p: dv_out.at[phase], dv_in.at[phase], dv_ss.at[phase], dv_rs.at[phase])

    def dots_end(phase):
        receive(
            "agg", lambda p: dv_out.at[phase], dv_in.at[phase], dv_ss.at[phase], dv_rs.at[phase]
        )
        total = jnp.sum(dv_in[phase], axis=0)[0:1]
        first = jnp.sum(jnp.where(line == case, total, 0.0), axis=1, keepdims=True)
        second = jnp.sum(jnp.where(line == case + cases, total, 0.0), axis=1, keepdims=True)
        return first, second

    step = 2 * depth

    def product(vector, matrix, low, high):
        @pl.loop(low, high)
        def _(c):
            at = pl.ds(pl.multiple_of(c * step, 128), step)
            local_ref[:, at] = dot(vector, matrix[:, at]) * mask_ref[0:1, at]

    chunks = order // step

    local_ref[...] = mask * dual_ref[...]
    pl.semaphore_wait(barrier, ns - 1 + na - 1)
    faces_start(0)

    across = lax.broadcasted_iota(jnp.int32, (primal, primal), 1)
    down = lax.broadcasted_iota(jnp.int32, (primal, primal), 0)
    owner_row = jnp.sum(
        jnp.where(across == down, owners_ref[...].astype(F32), 0.0), axis=0, keepdims=True
    )
    hot = jnp.where(
        lax.broadcasted_iota(jnp.int32, (8 * pl.cdiv(na, 8), primal), 0)
        == owner_row.astype(jnp.int32),
        1.0,
        0.0,
    )
    before = jnp.where(down < across, 1.0, 0.0).astype(BF16)
    earlier = dot(hot.astype(BF16), before)
    rank = jnp.sum(hot * earlier, axis=0, keepdims=True)
    late = rank >= half
    place_row = (
        owner_row * half + rank + jnp.where(late, float(used - half), 0.0)
    ).astype(jnp.int32)
    place_hot = jnp.where(
        lax.broadcasted_iota(jnp.int32, (2 * used, primal), 0) == place_row, 1.0, 0.0
    )
    place_col = jnp.sum(
        jnp.where(across == down, place_row.astype(F32), 0.0), axis=1, keepdims=True
    ).astype(jnp.int32)
    value_col = jnp.sum(
        jnp.where(across == down, rows_ref[...].astype(F32) + 1.0, 0.0), axis=1, keepdims=True
    )
    spot = lax.broadcasted_iota(jnp.int32, (primal, wide), 1) - agg * half
    fits = (spot >= 0) & (spot < half)
    tile_row = lax.broadcasted_iota(jnp.int32, (8, wide), 0)
    for o in range(na):
        tile = jnp.zeros((8, wide), F32)
        for h in range(2):
            match = fits & (place_col == spot + (h * used + o * half))
            ids = jnp.sum(jnp.where(match, value_col, 0.0), axis=0, keepdims=True)
            tile = tile + jnp.where(tile_row == h, ids, 0.0)
        ida_out[o] = tile
    ida_in[agg] = ida_out[agg]
    start("agg", lambda p: ida_out.at[p], ida_in, ida_ss, ida_rs)
    cp_ref[...] = dot(place_hot.astype(BF16), coupling_ref[...]).astype(BF16)
    b_in[...] = jnp.zeros_like(b_in)
    receive("agg", lambda p: ida_out.at[p], ida_in, ida_ss, ida_rs)
    mine = jnp.sum(ida_in[...], axis=0)
    idb_out[...] = mine
    idb_in[sub] = mine
    start("sub", lambda p: idb_out, idb_in, idb_ss, idb_rs)

    faces_end(0, residual_ref)

    load_d.wait()
    product(residual_ref[...].astype(BF16), dirichlet_ref, 0, chunks)
    rz = 2.0 * jnp.sum(residual_ref[...] * local_ref[...], axis=1, keepdims=True)
    faces_start(1)

    receive("sub", lambda p: idb_out, idb_in, idb_ss, idb_rs)
    coarse = coarse_ref[...]
    coarse_hi = coarse.astype(BF16)
    coarse_lo = (coarse - coarse_hi.astype(F32)).astype(BF16)
    both = jnp.concatenate([coarse_hi, coarse_lo], axis=0)
    index = lax.broadcasted_iota(jnp.int32, (nc, wide), 0).astype(F32) + 1.0

    @pl.loop(0, ns)
    def _(i):
        for h in range(2):
            chosen = jnp.where(index == idb_in[i, h : h + 1, :], 1.0, 0.0).astype(BF16)
            spread = dot(both, chosen).astype(BF16)
            at = pl.ds(pl.multiple_of(i * wide, 128), wide)
            hi_ref[h * crow : (h + 1) * crow, at] = spread[:crow]
            lo_ref[h * crow : (h + 1) * crow, at] = spread[crow:]

    fold = crow // 2
    held = ns * fold
    square = lax.broadcasted_iota(jnp.int32, (wide, wide), 0) == lax.broadcasted_iota(
        jnp.int32, (wide, wide), 1
    )
    at_lane = lax.broadcasted_iota(jnp.int32, (used, held), 1)
    number = (at_lane // fold) * crow + at_lane % fold + 1
    for h in range(2):
        ids = idb_out[h : h + 1, :]
        column = jnp.sum(jnp.where(square, ids, 0.0), axis=1, keepdims=True)
        column = column[:used].astype(jnp.int32)
        for g in range(2):
            found = jnp.where(number + g * fold == column, 1.0, 0.0)
            pick_ref[(2 * h + g) * used : (2 * h + g + 1) * used, :] = found.astype(BF16)

    faces_end(1, direction_ref)
    load_k.wait()

    for it in range(ITERS):
        vector = direction_ref[...].astype(BF16)
        terms = lax.dot_general(cp_ref[...], vector, NT, preferred_element_type=F32)
        out = jnp.concatenate([terms[:used], terms[used:]], axis=1)
        a_out[it] = out.reshape(na, half, 2 * cases)
        a_in[it, agg] = a_out[it, agg]
        start("agg", lambda p: a_out.at[it, p], a_in.at[it], a_ss.at[it], a_rs.at[it])
        product(vector, inverse_ref, 0, chunks // 2)
        receive("agg", lambda p: a_out.at[it, p], a_in.at[it], a_ss.at[it], a_rs.at[it])
        b_out[it] = a_in[it].reshape(used, 2 * cases)
        b_in[it, sub, 0:used] = b_out[it]

        def b_dst(j):
            return b_in.at[it, j, pl.ds(0, used)]

        @pl.loop(1, ns)
        def _(t):
            peer = lax.rem(sub + t, ns)
            pltpu.make_async_remote_copy(
                src_ref=b_out.at[it],
                dst_ref=b_dst(sub),
                send_sem=b_ss.at[it, t - 1],
                recv_sem=b_rs.at[it, t - 1],
                device_id={"sub": peer},
                device_id_type=MESH,
            ).start()

        product(vector, inverse_ref, chunks // 2, chunks)

        @pl.loop(1, ns)
        def _(t):
            peer = lax.rem(sub - t + ns, ns)
            copy = pltpu.make_async_remote_copy(
                src_ref=b_out.at[it],
                dst_ref=b_dst(peer),
                send_sem=b_ss.at[it, t - 1],
                recv_sem=b_rs.at[it, t - 1],
                device_id={"sub": peer},
                device_id_type=MESH,
            )
            copy.wait_recv()
            copy.wait_send()

        given = b_in[it].reshape(ns * wide, 2 * cases)
        given_hi = given.astype(BF16)
        given_lo = (given - given_hi.astype(F32)).astype(BF16)
        solved = (
            dot(hi_ref[...], given_hi) + dot(hi_ref[...], given_lo) + dot(lo_ref[...], given_hi)
        )
        rows = solved[:crow, :cases] + solved[crow:, cases:]
        s_out[it] = jnp.concatenate([rows[:fold], rows[fold:]], axis=1)
        s_in[it, sub] = s_out[it]
        start("sub", lambda p: s_out.at[it], s_in.at[it], s_ss.at[it], s_rs.at[it])
        receive("sub", lambda p: s_out.at[it], s_in.at[it], s_ss.at[it], s_rs.at[it])
        found = dot(pick_ref[...], s_in[it].reshape(held, 2 * cases).astype(BF16))
        answer = jnp.concatenate(
            [
                found[2 * h * used : (2 * h + 1) * used, :cases]
                + found[(2 * h + 1) * used : (2 * h + 2) * used, cases:]
                for h in range(2)
            ],
            axis=1,
        )
        r_out[it] = answer.reshape(na, half, 2 * cases)
        r_in[it, agg] = r_out[it, agg]
        start("agg", lambda p: r_out.at[it, p], r_in.at[it], r_ss.at[it], r_rs.at[it])
        receive("agg", lambda p: r_out.at[it, p], r_in.at[it], r_ss.at[it], r_rs.at[it])
        came = r_in[it].reshape(used, 2 * cases)
        back = jnp.concatenate([came[:, :cases], came[:, cases:]], axis=0)
        back = jnp.transpose(back).astype(BF16)

        @pl.loop(0, chunks)
        def _(c):
            at = pl.ds(pl.multiple_of(c * step, 128), step)
            local_ref[:, at] += dot(back, cp_ref[:, at]) * mask_ref[0:1, at]

        image_dot = 2.0 * jnp.sum(direction_ref[...] * local_ref[...], axis=1, keepdims=True)
        phase = 2 * it
        dots_start(phase, rz, image_dot)
        faces_start(2 + phase)
        dots_turn(phase)
        faces_end(2 + phase, field_ref)
        first, second = dots_end(phase)
        if it == 0:
            rz = first
        else:
            rz = rz_all
        alpha = rz / second
        if it == 0:
            solution_ref[...] = alpha * direction_ref[...]
        else:
            solution_ref[...] += alpha * direction_ref[...]
        residual_ref[...] -= alpha * field_ref[...]
        if it + 1 < ITERS:
            product(residual_ref[...].astype(BF16), dirichlet_ref, 0, chunks)
            part = 2.0 * jnp.sum(residual_ref[...] * local_ref[...], axis=1, keepdims=True)
            dots_start(phase + 1, part, part)
            faces_start(3 + phase)
            dots_turn(phase + 1)
            faces_end(3 + phase, field_ref)
            rz_all = dots_end(phase + 1)[0]
            direction_ref[...] = field_ref[...] + (rz_all / rz) * direction_ref[...]


def shards(
    dual_load,
    interface_inverse,
    dirichlet,
    coupling,
    neighbours,
    face_counts,
    owners,
    primal_rows,
    coarse_inverse,
):
    ns = lax.axis_size("sub")
    na = lax.axis_size("agg")
    reach = min(4, (ns - 1) // 2)
    cases, order = dual_load.shape[2:]
    slots = neighbours.shape[2]
    depth = order // slots
    crow, nc = coarse_inverse.shape[1:]
    half = CAP // 2
    used = na * half
    wide = pl.cdiv(used, 128) * 128
    lanes = 2 * cases
    face_rows = cases * depth // 128
    phases = 2 * ITERS + 1
    dots = 2 * ITERS - 1
    dma = pltpu.SemaphoreType.DMA

    def exchange(times, n, out, rows):
        return [
            pltpu.VMEM(out, F32),
            pltpu.VMEM(rows, F32),
            dma((times, n - 1) if times else (n - 1,)),
            dma((times, n - 1) if times else (n - 1,)),
        ]

    scratch = [
        pltpu.VMEM((order, order), BF16),
        pltpu.VMEM((order, order), BF16),
        pltpu.VMEM((cases, order), F32),
        pltpu.VMEM((cases, order), F32),
        pltpu.VMEM((cases, order), F32),
        pltpu.VMEM((slots, face_rows, 128), F32),
        pltpu.VMEM((phases, 2 * reach, face_rows, 128), F32),
        pltpu.VMEM((phases, 2 * reach, face_rows, 128), F32),
        dma((phases, 2 * reach)),
        dma((phases, 2 * reach)),
        dma((2,)),
        pltpu.VMEM((2 * used, order), BF16),
        pltpu.VMEM((8, order), F32),
        *exchange(0, na, (na, 8, wide), (na, 8, wide)),
        *exchange(0, ns, (8, wide), (ns, 8, wide)),
        pltpu.VMEM((2 * crow, ns * wide), BF16),
        pltpu.VMEM((2 * crow, ns * wide), BF16),
        pltpu.VMEM((4 * used, ns * crow // 2), BF16),
        *exchange(ITERS, na, (ITERS, na, half, lanes), (ITERS, na, half, lanes)),
        *exchange(ITERS, ns, (ITERS, used, lanes), (ITERS, ns, wide, lanes)),
        *exchange(ITERS, ns, (ITERS, crow // 2, lanes), (ITERS, ns, crow // 2, lanes)),
        *exchange(ITERS, na, (ITERS, na, half, lanes), (ITERS, na, half, lanes)),
        *exchange(dots, ns, (dots, 8, lanes), (dots, ns, 8, lanes)),
        *exchange(dots, na, (dots, 8, lanes), (dots, na, 8, lanes)),
    ]
    vmem = pl.BlockSpec(memory_space=pltpu.VMEM)
    smem = pl.BlockSpec(memory_space=pltpu.SMEM)
    anywhere = pl.BlockSpec(memory_space=pl.ANY)
    shape = jax.ShapeDtypeStruct((cases, order), F32)
    solved, left = pl.pallas_call(
        functools.partial(kernel, ns, na, reach),
        out_shape=(shape, shape),
        in_specs=[vmem, anywhere, anywhere, vmem, smem, smem, vmem, vmem, vmem],
        out_specs=(vmem, vmem),
        scratch_shapes=scratch,
        compiler_params=pltpu.CompilerParams(
            collective_id=0, has_side_effects=True, vmem_limit_bytes=56 * 1024 * 1024
        ),
    )(
        dual_load[0, 0],
        interface_inverse[0, 0],
        dirichlet[0, 0],
        coupling[0, 0],
        neighbours[0, 0],
        face_counts[0, 0],
        owners[0, 0],
        primal_rows[0],
        coarse_inverse[0],
    )
    return solved[None, None], left[None, None]


def solution(mesh):
    in_specs = (
        P("agg", "sub", None, None),
        P("agg", "sub", None, None),
        P("agg", "sub", None, None),
        P("agg", "sub", None, None),
        P("agg", "sub", None),
        P("agg", "sub", None),
        P("agg", "sub", None, None),
        P("agg", "sub", None),
        P("agg", "sub", None),
    )
    out_specs = (P("agg", "sub", None, None), P("agg", "sub", None, None))
    return jax.shard_map(shards, mesh=mesh, in_specs=in_specs, out_specs=out_specs, check_vma=False)
```

time: 560 us -> 114 us (0.20)
  blocking collectives: 198 us -> 0 us
  waiting for transfers between devices: 149 us -> 0 us
  Pallas kernels: 0 us -> 108 us
  local copies, waits for them, and re-layouts: 76.6 us -> 4.93 us
  starting transfers between devices: 58.8 us -> 0 us
  other arithmetic: 32.5 us -> 0 us
  matrix products: 27.5 us -> 0 us
  between operations: 14.8 us -> 0.64 us
    psum x2 -> x0, waiting for transfers between devices: 142 us -> none  [shards(): coarse_rhs = lax.psum(gathered, 'sub')]
    psum x3 -> x0, blocking collectives: 115 us -> none  [the longest x2 77.8 us: residual_norm(): return lax.psum(jnp.sum(first * second, axis=1), ('sub', 'agg'))]
    pallas_call x0 -> x1, Pallas kernels: none -> 108 us  [shards(): pl.pallas_call(functools.partial(kernel, ns, na, reach), out_shape=(shape...]
    mul x78 -> x0, local copies, waits for them, and re-layouts: 64.3 us -> none  [the longest x39 32.2 us: assemble(): to_behind * from_behind[:, None, :]]
    all_gather x2 -> x0, blocking collectives: 61.7 us -> none  [shards(): coarse_sol = lax.all_gather(partial_rows, 'sub', axis=1, tiled=True)]
    ppermute x30 -> x0, starting transfers between devices: 51.8 us -> none  [from_behind_2(): return lax.ppermute(block, axis, route)]
    dot_general x18 -> x0, matrix products: 27.5 us -> none  [the longest x2 7.35 us: precondition(): jnp.dot(packed, dirichlet_block, preferred_element_type=jnp.float32)]
    all_to_all x3 -> x0, blocking collectives: 20.5 us -> none  [the longest x2 13.1 us: shards(): lax.all_to_all(answer, 'agg', split_axis=1, concat_axis=1, tiled=True)]
  transfers between devices with their start and end apart: 34 -> 0, of which waited for: 8 -> 0; matrix products, arithmetic and copies ran while one was open for 12% -> 0% of each run, Pallas kernels for 0% -> 0%
where the time goes in v1:
time: 114 us; the launch traced here: 113 us
  Pallas kernels  108 us (95%)
  local copies, waits for them, and re-layouts  4.93 us (4%)
    pallas_call x1, Pallas kernels, shards(): pl.pallas_call(functools.partial(kernel, ns, na, reach), out_shape=(shape...  108 us
    unnamed x2, local copies, waits for them, and re-layouts  3.54 us

profile of v1, /device:TPU:0, one launch (start us, length us, event | category | flops | bytes accessed | tf_op | source)
XLA Modules:
  0.0 113.4 jit_solution(15601369853530374572)
XLA Ops:
  0.6 1.4 %copy.11.owners_ref = s32[128,1]{1,0:T(8,128)} copy(s32[128,1]{0,1:T(1,128)} %bitcast.18) | data formatting | bytes 1024 | tf_op jit(solution)/shard_map/squeeze | solution.py:531
  2.0 107.8 %shard_map.104 = (f32[64,1536]{1,0:T(8,128)}, f32[64,1536]{1,0:T(8,128)}) custom-call(f32[64,1536]{1,0:T(8,128)} %bitcast.14, bf16[1536,1536]{1,0:T(8,128)(2,1)} %bitcast.11, bf16[1536,1536]{1,0:T(8,128)(2,1)} %bitcast.12, bf16[128,1536]{1,0:T(8,128)(2,1)} %bitcast.15, s32[8]{0:T(128)} %bitcast.19, s32[8]{0:T(128)} %bitcast.20, s32[128,1]{1,0:T(8,128)} %copy.11.owners_ref, ...), custom_call_target="tpu_custom_call" | custom-call | tf_op jit(solution)/shard_map/pallas_call | solution.py:515
  109.9 1.8 %copy.14 = f32[1,1,64,1536]{3,2,1,0:T(8,128)} copy(f32[1,1,64,1536]{3,2,1,0:T(8,128)} %bitcast.17) | data formatting | bytes 786432
  111.6 1.8 %copy.15 = f32[1,1,64,1536]{3,2,1,0:T(8,128)} copy(f32[1,1,64,1536]{3,2,1,0:T(8,128)} %bitcast.16) | data formatting | bytes 786432

commit v2 on v1

--- a/solution.py
+++ b/solution.py
@@ -146,6 +146,52 @@
             copy.wait_recv()
             copy.wait_send()
 
+    pairs = ns // 2
+    pair, parity = lax.div(sub, 2), lax.rem(sub, 2)
+
+    def ahead_of(t):
+        return 2 * lax.rem(pair + t, pairs) + parity
+
+    def behind(t, side):
+        return 2 * lax.rem(pair - t + pairs, pairs) + side
+
+    def leg(src, dst, k, ss, rs, to):
+        return pltpu.make_async_remote_copy(
+            src_ref=src,
+            dst_ref=dst,
+            send_sem=ss.at[k],
+            recv_sem=rs.at[k],
+            device_id={"sub": to},
+            device_id_type=MESH,
+        )
+
+    partner = 2 * pair + 1 - parity
+
+    def spread_start(src, dst_of, ss, rs):
+        @pl.loop(1, pairs)
+        def _(t):
+            leg(src, dst_of(sub), t - 1, ss, rs, ahead_of(t)).start()
+
+        leg(src, dst_of(sub), pairs - 1, ss, rs, partner).start()
+
+    def spread_end(src, dst_of, ss, rs):
+        @pl.loop(1, pairs)
+        def _(t):
+            block = dst_of(behind(t, parity))
+            leg(src, block, t - 1, ss, rs, ahead_of(t)).wait_recv()
+            leg(block, block, pairs - 1 + t, ss, rs, partner).start()
+
+        leg(src, dst_of(partner), pairs - 1, ss, rs, partner).wait_recv()
+
+        @pl.loop(1, pairs)
+        def _(t):
+            block = dst_of(behind(t, 1 - parity))
+            leg(src, block, pairs - 1 + t, ss, rs, partner).wait_recv()
+
+        @pl.loop(0, 2 * pairs - 1)
+        def _(k):
+            leg(src, dst_of(sub), k, ss, rs, partner).wait_send()
+
     barrier = pltpu.get_barrier_semaphore()
     for axis, me, n in (("sub", sub, ns), ("agg", agg, na)):
 
@@ -170,9 +216,9 @@
     hops = []
     for distance in range(1, reach + 1):
         ahead = lax.rem(sub + distance, ns)
-        behind = lax.rem(sub + ns - distance, ns)
-        hops.append((ahead, behind))
-        hops.append((behind, ahead))
+        back = lax.rem(sub + ns - distance, ns)
+        hops.append((ahead, back))
+        hops.append((back, ahead))
     weights = [
         [jnp.where(peers_ref[k] == to, 1.0, 0.0) for k in range(slots)] for to, _ in hops
     ]
@@ -241,7 +287,7 @@
         second = jnp.sum(jnp.where(line == case + cases, total, 0.0), axis=1, keepdims=True)
         return first, second
 
-    step = 2 * depth
+    step = next(w for w in (512, 384, 256, 128, order) if order % w == 0)
 
     def product(vector, matrix, low, high):
         @pl.loop(low, high)
@@ -257,9 +303,7 @@
 
     across = lax.broadcasted_iota(jnp.int32, (primal, primal), 1)
     down = lax.broadcasted_iota(jnp.int32, (primal, primal), 0)
-    owner_row = jnp.sum(
-        jnp.where(across == down, owners_ref[...].astype(F32), 0.0), axis=0, keepdims=True
-    )
+    owner_row = owners_ref[...].astype(F32)
     hot = jnp.where(
         lax.broadcasted_iota(jnp.int32, (8 * pl.cdiv(na, 8), primal), 0)
         == owner_row.astype(jnp.int32),
@@ -318,12 +362,19 @@
 
     @pl.loop(0, ns)
     def _(i):
+        chosen = jnp.concatenate(
+            [
+                jnp.where(index == idb_in[i, h : h + 1, :], 1.0, 0.0).astype(BF16)
+                for h in range(2)
+            ],
+            axis=1,
+        )
+        spread = dot(both, chosen).astype(BF16)
+        at = pl.ds(pl.multiple_of(i * wide, 128), wide)
         for h in range(2):
-            chosen = jnp.where(index == idb_in[i, h : h + 1, :], 1.0, 0.0).astype(BF16)
-            spread = dot(both, chosen).astype(BF16)
-            at = pl.ds(pl.multiple_of(i * wide, 128), wide)
-            hi_ref[h * crow : (h + 1) * crow, at] = spread[:crow]
-            lo_ref[h * crow : (h + 1) * crow, at] = spread[crow:]
+            part = spread[:, h * wide : (h + 1) * wide]
+            hi_ref[h * crow : (h + 1) * crow, at] = part[:crow]
+            lo_ref[h * crow : (h + 1) * crow, at] = part[crow:]
 
     fold = crow // 2
     held = ns * fold
@@ -358,34 +409,10 @@
         def b_dst(j):
             return b_in.at[it, j, pl.ds(0, used)]
 
-        @pl.loop(1, ns)
-        def _(t):
-            peer = lax.rem(sub + t, ns)
-            pltpu.make_async_remote_copy(
-                src_ref=b_out.at[it],
-                dst_ref=b_dst(sub),
-                send_sem=b_ss.at[it, t - 1],
-                recv_sem=b_rs.at[it, t - 1],
-                device_id={"sub": peer},
-                device_id_type=MESH,
-            ).start()
-
+        spread_start(b_out.at[it], b_dst, b_ss.at[it], b_rs.at[it])
         product(vector, inverse_ref, chunks // 2, chunks)
 
-        @pl.loop(1, ns)
-        def _(t):
-            peer = lax.rem(sub - t + ns, ns)
-            copy = pltpu.make_async_remote_copy(
-                src_ref=b_out.at[it],
-                dst_ref=b_dst(peer),
-                send_sem=b_ss.at[it, t - 1],
-                recv_sem=b_rs.at[it, t - 1],
-                device_id={"sub": peer},
-                device_id_type=MESH,
-            )
-            copy.wait_recv()
-            copy.wait_send()
-
+        spread_end(b_out.at[it], b_dst, b_ss.at[it], b_rs.at[it])
         given = b_in[it].reshape(ns * wide, 2 * cases)
         given_hi = given.astype(BF16)
         given_lo = (given - given_hi.astype(F32)).astype(BF16)
@@ -395,8 +422,12 @@
         rows = solved[:crow, :cases] + solved[crow:, cases:]
         s_out[it] = jnp.concatenate([rows[:fold], rows[fold:]], axis=1)
         s_in[it, sub] = s_out[it]
-        start("sub", lambda p: s_out.at[it], s_in.at[it], s_ss.at[it], s_rs.at[it])
-        receive("sub", lambda p: s_out.at[it], s_in.at[it], s_ss.at[it], s_rs.at[it])
+
+        def s_dst(j):
+            return s_in.at[it, j]
+
+        spread_start(s_out.at[it], s_dst, s_ss.at[it], s_rs.at[it])
+        spread_end(s_out.at[it], s_dst, s_ss.at[it], s_rs.at[it])
         found = dot(pick_ref[...], s_in[it].reshape(held, 2 * cases).astype(BF16))
         answer = jnp.concatenate(
             [
@@ -528,7 +559,7 @@
         coupling[0, 0],
         neighbours[0, 0],
         face_counts[0, 0],
-        owners[0, 0],
+        owners[0, 0].reshape(1, -1),
         primal_rows[0],
         coarse_inverse[0],
     )

time: 114 us -> 110 us (0.965)
  Pallas kernels: 108 us -> 106 us
  local copies, waits for them, and re-layouts: 4.93 us -> 3.54 us
    pallas_call x1, Pallas kernels: 108 us -> 106 us  [shards(): pl.pallas_call(functools.partial(kernel, ns, na, reach), out_shape=(shape...]
    squeeze x1 -> x0, local copies, waits for them, and re-layouts: 1.39 us -> none  [shards(): owners[0, 0]]
where the time goes in v2:
time: 110 us
  Pallas kernels  106 us (96%)
  local copies, waits for them, and re-layouts  3.54 us (3%)
    pallas_call x1, Pallas kernels, shards(): pl.pallas_call(functools.partial(kernel, ns, na, reach), out_shape=(shape...  106 us
    unnamed x2, local copies, waits for them, and re-layouts  3.54 us

profile of v2, /device:TPU:0, one launch (start us, length us, event | category | flops | bytes accessed | tf_op | source)
XLA Modules:
  0.0 110.2 jit_solution(7307687341543959134)
XLA Ops:
  0.6 106.0 %shard_map.104 = (f32[64,1536]{1,0:T(8,128)}, f32[64,1536]{1,0:T(8,128)}) custom-call(f32[64,1536]{1,0:T(8,128)} %bitcast.14, bf16[1536,1536]{1,0:T(8,128)(2,1)} %bitcast.11, bf16[1536,1536]{1,0:T(8,128)(2,1)} %bitcast.12, bf16[128,1536]{1,0:T(8,128)(2,1)} %bitcast.15, s32[8]{0:T(128)} %bitcast.18, s32[8]{0:T(128)} %bitcast.19, s32[1,128]{1,0:T(1,128)} %bitcast.20, ...), custom_call_target="tpu_custom_call" | custom-call | tf_op jit(solution)/shard_map/pallas_call | solution.py:546
  106.6 1.8 %copy.13 = f32[1,1,64,1536]{3,2,1,0:T(8,128)} copy(f32[1,1,64,1536]{3,2,1,0:T(8,128)} %bitcast.17) | data formatting | bytes 786432
  108.4 1.8 %copy.14 = f32[1,1,64,1536]{3,2,1,0:T(8,128)} copy(f32[1,1,64,1536]{3,2,1,0:T(8,128)} %bitcast.16) | data formatting | bytes 786432

commit v3 on v2

--- a/solution.py
+++ b/solution.py
@@ -114,6 +114,8 @@
     sub = lax.axis_index("sub")
     agg = lax.axis_index("agg")
 
+    unsent = []
+
     def start(axis, src_of, dst, ss, rs):
         me, n = (sub, ns) if axis == "sub" else (agg, na)
 
@@ -132,10 +134,9 @@
     def receive(axis, src_of, dst, ss, rs):
         me, n = (sub, ns) if axis == "sub" else (agg, na)
 
-        @pl.loop(1, n)
-        def _(t):
+        def copy(t):
             peer = lax.rem(me - t + n, n)
-            copy = pltpu.make_async_remote_copy(
+            return pltpu.make_async_remote_copy(
                 src_ref=src_of(peer),
                 dst_ref=dst.at[peer],
                 send_sem=ss.at[t - 1],
@@ -143,8 +144,17 @@
                 device_id={axis: peer},
                 device_id_type=MESH,
             )
-            copy.wait_recv()
-            copy.wait_send()
+
+        @pl.loop(1, n)
+        def _(t):
+            copy(t).wait_recv()
+
+        def sent():
+            @pl.loop(1, n)
+            def _(t):
+                copy(t).wait_send()
+
+        unsent.append(sent)
 
     pairs = ns // 2
     pair, parity = lax.div(sub, 2), lax.rem(sub, 2)
@@ -188,9 +198,12 @@
             block = dst_of(behind(t, 1 - parity))
             leg(src, block, pairs - 1 + t, ss, rs, partner).wait_recv()
 
-        @pl.loop(0, 2 * pairs - 1)
-        def _(k):
-            leg(src, dst_of(sub), k, ss, rs, partner).wait_send()
+        def sent():
+            @pl.loop(0, 2 * pairs - 1)
+            def _(k):
+                leg(src, dst_of(sub), k, ss, rs, partner).wait_send()
+
+        unsent.append(sent)
 
     barrier = pltpu.get_barrier_semaphore()
     for axis, me, n in (("sub", sub, ns), ("agg", agg, na)):
@@ -245,7 +258,8 @@
 
     def faces_end(phase, out_ref):
         for e in range(len(hops)):
-            face_copy(phase, e).wait()
+            face_copy(phase, e).wait_recv()
+            unsent.append(face_copy(phase, e).wait_send)
         for k in range(0, slots, 2):
             pair = []
             for j in (k, k + 1):
@@ -400,13 +414,13 @@
         out = jnp.concatenate([terms[:used], terms[used:]], axis=1)
         a_out[it] = out.reshape(na, half, 2 * cases)
         a_in[it, agg] = a_out[it, agg]
-        start("agg", lambda p: a_out.at[it, p], a_in.at[it], a_ss.at[it], a_rs.at[it])
+        start("agg", lambda p, it=it: a_out.at[it, p], a_in.at[it], a_ss.at[it], a_rs.at[it])
         product(vector, inverse_ref, 0, chunks // 2)
-        receive("agg", lambda p: a_out.at[it, p], a_in.at[it], a_ss.at[it], a_rs.at[it])
+        receive("agg", lambda p, it=it: a_out.at[it, p], a_in.at[it], a_ss.at[it], a_rs.at[it])
         b_out[it] = a_in[it].reshape(used, 2 * cases)
         b_in[it, sub, 0:used] = b_out[it]
 
-        def b_dst(j):
+        def b_dst(j, it=it):
             return b_in.at[it, j, pl.ds(0, used)]
 
         spread_start(b_out.at[it], b_dst, b_ss.at[it], b_rs.at[it])
@@ -423,7 +437,7 @@
         s_out[it] = jnp.concatenate([rows[:fold], rows[fold:]], axis=1)
         s_in[it, sub] = s_out[it]
 
-        def s_dst(j):
+        def s_dst(j, it=it):
             return s_in.at[it, j]
 
         spread_start(s_out.at[it], s_dst, s_ss.at[it], s_rs.at[it])
@@ -439,8 +453,8 @@
         )
         r_out[it] = answer.reshape(na, half, 2 * cases)
         r_in[it, agg] = r_out[it, agg]
-        start("agg", lambda p: r_out.at[it, p], r_in.at[it], r_ss.at[it], r_rs.at[it])
-        receive("agg", lambda p: r_out.at[it, p], r_in.at[it], r_ss.at[it], r_rs.at[it])
+        start("agg", lambda p, it=it: r_out.at[it, p], r_in.at[it], r_ss.at[it], r_rs.at[it])
+        receive("agg", lambda p, it=it: r_out.at[it, p], r_in.at[it], r_ss.at[it], r_rs.at[it])
         came = r_in[it].reshape(used, 2 * cases)
         back = jnp.concatenate([came[:, :cases], came[:, cases:]], axis=0)
         back = jnp.transpose(back).astype(BF16)
@@ -476,6 +490,9 @@
             faces_end(3 + phase, field_ref)
             rz_all = dots_end(phase + 1)[0]
             direction_ref[...] = field_ref[...] + (rz_all / rz) * direction_ref[...]
+
+    for sent in unsent:
+        sent()
 
 
 def shards(

time: 110 us -> 111 us (level)
  no operation moved by 1% of the time
where the time goes in v3:
time: 111 us
  Pallas kernels  106 us (95%)
  local copies, waits for them, and re-layouts  3.54 us (3%)
    pallas_call x1, Pallas kernels, shards(): pl.pallas_call(functools.partial(kernel, ns, na, reach), out_shape=(shape...  106 us
    unnamed x2, local copies, waits for them, and re-layouts  3.54 us

profile of v3, /device:TPU:0, one launch (start us, length us, event | category | flops | bytes accessed | tf_op | source)
XLA Modules:
  0.0 110.7 jit_solution(13771767892405247099)
XLA Ops:
  0.6 106.5 %shard_map.104 = (f32[64,1536]{1,0:T(8,128)}, f32[64,1536]{1,0:T(8,128)}) custom-call(f32[64,1536]{1,0:T(8,128)} %bitcast.14, bf16[1536,1536]{1,0:T(8,128)(2,1)} %bitcast.11, bf16[1536,1536]{1,0:T(8,128)(2,1)} %bitcast.12, bf16[128,1536]{1,0:T(8,128)(2,1)} %bitcast.15, s32[8]{0:T(128)} %bitcast.18, s32[8]{0:T(128)} %bitcast.19, s32[1,128]{1,0:T(1,128)} %bitcast.20, ...), custom_call_target="tpu_custom_call" | custom-call | tf_op jit(solution)/shard_map/pallas_call | solution.py:563
  107.1 1.8 %copy.13 = f32[1,1,64,1536]{3,2,1,0:T(8,128)} copy(f32[1,1,64,1536]{3,2,1,0:T(8,128)} %bitcast.17) | data formatting | bytes 786432
  108.9 1.8 %copy.14 = f32[1,1,64,1536]{3,2,1,0:T(8,128)} copy(f32[1,1,64,1536]{3,2,1,0:T(8,128)} %bitcast.16) | data formatting | bytes 786432
